TPU v7x, 512 devices: a whole 4x4x16 slice. The times are simulated.
512 devices in a mesh: row: 16 (over y_hi, x, core), col: 32 (over y_lo, z).
Axes of the slice: x: 4, y: 4 (y_hi: 2, y_lo: 2; y = y_hi * 2 + y_lo), z: 16, core: 2. Of those that a mesh axis runs over, the one named last changes fastest.
Arguments:
- amp_packed: float32 [6144, 3072], P('row', 'col'), may hold values from -6 to 6
- pair_rows: int32 [6144], P('row'), may hold values from 0 to 6143, as said below
- integrals: float32 [3072, 24576], P('row', 'col'), may hold values from -0.109375 to 0.109375
Outputs:
- ladder: float32 [6144, 24576], P('row', 'col')
Inputs may be any that keep to these rules, and one draw needn't show every extreme that they name: `pair_rows`: A permutation of the 6144 matrix rows. Each aligned block of 384 storage positions holds exactly 24 rows of every aligned block of 384 matrix rows.
All inputs are finite; a program needn't handle non-finite values.
Results may differ from a plain program's by a relative error of at most 0.00007.
Values sent between devices are 32-bit elements; how exact they have to be, the bound alone decides.
No kernel may reach another device: no remote copies, remote signals or barrier semaphores. Data moves between devices by JAX's collectives and lax.ppermute only.
A program may use at most 64 MiB of HBM per device.

v0:
```python
import jax
import jax.numpy as jnp
from jax import lax
from jax.sharding import PartitionSpec as P


def sorted_outgoing(values, targets):
    count = values.shape[0]
    block = targets // count
    order = jnp.argsort(block, stable=True)
    return (values[order], (targets % count)[order])


def local(amp_packed, pair_rows, integrals):
    outgoing, places = sorted_outgoing(amp_packed, pair_rows)
    arrived, spots = (
        lax.all_to_all(outgoing, "row", split_axis=0, concat_axis=0, tiled=True),
        lax.all_to_all(places, "row", split_axis=0, concat_axis=0, tiled=True),
    )
    local_amp = arrived[jnp.argsort(spots)]
    full_amp = lax.all_gather(local_amp, "col", axis=1, tiled=True)
    full_ints = lax.all_gather(integrals, "row", axis=0, tiled=True)
    result = jnp.dot(
        full_amp, full_ints, preferred_element_type=jnp.float32, precision=lax.Precision.HIGHEST
    )
    return result


def solution(mesh):
    in_specs = (P("row", "col"), P("row"), P("row", "col"))
    out_specs = P("row", "col")
    return jax.shard_map(local, mesh=mesh, in_specs=in_specs, out_specs=out_specs, check_vma=False)
```

profile of v0, /device:TPU:1, one launch (start us, length us, event | category | flops | bytes accessed | tf_op | source)
XLA Modules:
  0.0 296.6 jit_solution(15111412111634310055)
XLA Ops:
  6.5 0.7 add_select_fusion
  7.2 3.8 %sort.34 = (s32[384]{0:T(512)}, s32[384]{0:T(512)S(1)}) sort(s32[384]{0:T(512)S(1)} %get-tuple-element.10, s32[384]{0:T(512)S(1)} %iota.8), dimensions={0}, to_apply=%region_0.1 | sort | flops 3456 | bytes 6144 | tf_op jit(solution)/shard_map/jit(argsort)/sort | solution.py:10
  11.0 2.8 gather_fusion.1
  13.8 0.7 all_to_all.19
  14.5 10.2 %all-to-all-start.1 = ((s32[16,24,1]{1,2,0:T(1,128)}), s32[16,24,1]{1,2,0:T(1,128)S(1)}, u32[]{:S(2)}, u32[]{:S(2)}) async-start(s32[16,24,1]{1,2,0:T(1,128)} %bitcast.2), calls=%async_computation.1 | async-start | bytes 16384 | tf_op jit(solution)/shard_map/all_to_all | solution.py:18
  24.7 1.0 copy.6
  25.7 1.6 gather_fusion
  27.3 4.4 %all-to-all-done.1 = s32[16,24,1]{1,2,0:T(1,128)S(1)} async-done(((s32[16,24,1]{1,2,0:T(1,128)}), s32[16,24,1]{1,2,0:T(1,128)S(1)}, u32[]{:S(2)}, u32[]{:S(2)}) %all-to-all-start.1) | async-done | bytes 1568 | tf_op jit(solution)/shard_map/all_to_all | solution.py:18
  31.7 3.8 %all-to-all-start = ((f32[16,24,96]{2,1,0:T(8,128)}), f32[16,24,96]{2,1,0:T(8,128)S(1)}, u32[]{:S(2)}, u32[]{:S(2)}) async-start(f32[16,24,96]{2,1,0:T(8,128)} %bitcast), calls=%async_computation | async-start | bytes 393216 | tf_op jit(solution)/shard_map/all_to_all | solution.py:17
  35.6 0.0 all-gather.6.cloned.1.call-start
  35.6 0.6 broadcast.18
  36.2 0.7 reduce.3
  36.9 0.1 all_to_all.21
  37.0 3.8 %sort.35 = (s32[384]{0:T(512)}, s32[384]{0:T(512)S(1)}) sort(s32[384]{0:T(512)S(1)} %all_to_all.21, s32[384]{0:T(512)S(1)} %iota.9), dimensions={0}, to_apply=%region_1.2 | sort | flops 3456 | bytes 6144 | tf_op jit(solution)/shard_map/jit(argsort)/sort | solution.py:20
  40.8 3.0 %all-to-all-done = f32[16,24,96]{2,1,0:T(8,128)S(1)} async-done(((f32[16,24,96]{2,1,0:T(8,128)}), f32[16,24,96]{2,1,0:T(8,128)S(1)}, u32[]{:S(2)}, u32[]{:S(2)}) %all-to-all-start) | async-done | bytes 147488 | tf_op jit(solution)/shard_map/all_to_all | solution.py:17
  43.8 1.1 gather_fusion.2
  44.9 0.8 copy.8
  45.7 0.0 all-gather.6.cloned.1.call-update
  45.7 0.0 all-gather.4.cloned.1.call-start
  45.8 0.7 all-gather.4.cloned.1.call-update
  46.5 121.4 %all-gather.6.cloned.1.call-done = f32[384,3072]{0,1:T(8,128)} async-done(((f32[384,96]{0,1:T(8,128)}), f32[384,3072]{0,1:T(8,128)}) %all-gather.6.cloned.1.call-update) | async-done | bytes 4718608 | tf_op jit(solution)/shard_map/all_gather | solution.py:21
  167.9 106.4 %all-gather.4.cloned.1.call-done = f32[3072,768]{1,0:T(8,128)} async-done(((f32[192,768]{1,0:T(8,128)}), f32[3072,768]{1,0:T(8,128)}) %all-gather.4.cloned.1.call-update) | async-done | bytes 9437200 | tf_op jit(solution)/shard_map/all_gather | solution.py:22
  274.2 15.6 %fusion.1 = f32[384,768]{1,0:T(8,128)} fusion(f32[384,3072]{0,1:T(8,128)} %all-gather.6.cloned.1.call-done, f32[3072,768]{1,0:T(8,128)} %all-gather.4.cloned.1.call-done), kind=kOutput, calls=%fused_computation.12 | convolution fusion | flops 10871635968 | bytes 15335424 | tf_op jit(solution)/shard_map/dot_general | solution.py:23
  (6 shorter events, 0.0 us)
Async XLA Ops:
  14.5 17.2 %all-to-all-start.1 = ((s32[16,24,1]{1,2,0:T(1,128)}), s32[16,24,1]{1,2,0:T(1,128)S(1)}, u32[]{:S(2)}, u32[]{:S(2)}) async-start(s32[16,24,1]{1,2,0:T(1,128)} %bitcast.2), calls=%async_computation.1 | async-start | bytes 16384 | tf_op jit(solution)/shard_map/all_to_all | solution.py:18
  31.7 12.1 %all-to-all-start = ((f32[16,24,96]{2,1,0:T(8,128)}), f32[16,24,96]{2,1,0:T(8,128)S(1)}, u32[]{:S(2)}, u32[]{:S(2)}) async-start(f32[16,24,96]{2,1,0:T(8,128)} %bitcast), calls=%async_computation | async-start | bytes 393216 | tf_op jit(solution)/shard_map/all_to_all | solution.py:17
  35.6 132.3 %all-gather.6.cloned.1.call-start = ((), (), s32[]{:S(2)}) async-start(), calls=%async_computation.3 | async-start | bytes 4866048 | tf_op jit(solution)/shard_map/all_gather | solution.py:21
  45.7 228.5 %all-gather.4.cloned.1.call-start = ((), (), s32[]{:S(2)}) async-start(), calls=%async_computation.2 | async-start | bytes 10027008 | tf_op jit(solution)/shard_map/all_gather | solution.py:22
Sparse Core Ops, SparseCore 0:
  45.8 121.9 all-gather.5
  171.2 103.0 all-gather.3
where the time goes:
time: 297 us
  waiting for transfers between devices  236 us (79%)
  matrix products  15.6 us (5%)
  starting transfers between devices  14.1 us (5%)
  between operations  13.5 us (5%)
  other arithmetic  8.98 us (3%)
  local copies, waits for them, and re-layouts  8.73 us (3%)
    all_gather x1, waiting for transfers between devices, local(): full_amp = lax.all_gather(local_amp, 'col', axis=1, tiled=True)  121 us
    all_gather x1, waiting for transfers between devices, local(): full_ints = lax.all_gather(integrals, 'row', axis=0, tiled=True)  106 us
    dot_general x1, matrix products, local(): jnp.dot(full_amp, full_ints, preferred_element_type=jnp.float32, precisio...  15.6 us
    all_to_all x1, starting transfers between devices, local(): lax.all_to_all(places, 'row', split_axis=0, concat_axis=0, tiled=True)  10.2 us
  transfers between devices with their start and end apart: 4, of which 4 were waited for; matrix products, arithmetic and copies ran while one was open for 3% of the time, Pallas kernels for 0%

commit v1 on v0

v1 whole, which is shorter than its diff:
```python
import jax
import jax.numpy as jnp
from jax import lax
from jax.experimental import pallas as pl
from jax.experimental.pallas import tpu as pltpu
from jax.sharding import Mesh, PartitionSpec as P

F32 = jnp.float32
BF16 = jnp.bfloat16
ROWS = 384
KB = 96
COLS = 768
KR = 192
CD = 3072
SEND = 24


def exact_pick(onehot, values):
    hi = values.astype(BF16)
    rest = values - hi.astype(F32)
    mid = rest.astype(BF16)
    lo = (rest - mid.astype(F32)).astype(BF16)
    dot = lambda part: jnp.dot(onehot, part, preferred_element_type=F32)
    return (dot(hi) + dot(mid)) + dot(lo)


def pack_kernel(rows_ref, own_ref, other_ref, out_ref):
    rows = rows_ref[...]
    block = ((rows >> 7) * 171) >> 9
    place = rows - block * ROWS
    down = lax.broadcasted_iota(jnp.int32, (ROWS, ROWS), 0)
    along = lax.broadcasted_iota(jnp.int32, (ROWS, ROWS), 1)
    block_f = block.astype(F32)
    diagonal = down == along
    column = lambda v: jnp.sum(jnp.where(diagonal, v, 0.0), axis=1, keepdims=True)
    same = (column(block_f) == block_f) & (down < along)
    rank = jnp.sum(jnp.where(same, 1.0, 0.0), axis=0, keepdims=True)
    position = block_f * float(SEND) + rank
    onehot = jnp.where(down.astype(F32) == position, 1.0, 0.0).astype(BF16)
    places = jnp.broadcast_to(column(place.astype(F32)), (ROWS, 32))
    values = jnp.concatenate([own_ref[...].T, places, other_ref[...].T, places], axis=1)
    out_ref[...] = exact_pick(onehot, values)


def unpack_kernel(arrived_ref, out_ref):
    arrived = arrived_ref[...]
    places = arrived[:, KB : KB + 1]
    along = lax.broadcasted_iota(jnp.int32, (ROWS, ROWS), 1).astype(F32)
    onehot = jnp.where(along == places, 1.0, 0.0).astype(BF16)
    flipped = arrived.T
    hi = flipped.astype(BF16)
    rest = flipped - hi.astype(F32)
    mid = rest.astype(BF16)
    lo = (rest - mid.astype(F32)).astype(BF16)
    dot = lambda part: jnp.dot(part, onehot, preferred_element_type=F32)
    placed = (dot(hi) + dot(mid)) + dot(lo)
    out_ref[:KB, :] = placed[:KB]
    out_ref[KB:, :] = placed[128 : 128 + KB]


def split(v):
    hi = v.astype(BF16)
    return hi, (v - hi.astype(F32)).astype(BF16)


def multiply_kernel(where_ref, amp_ref, mine_ref, twin_ref, out_ref, amp, ints, amp_sem, ints_sem):
    n_amp = 2 * 16
    core = where_ref[0]
    amp_copies = [
        pltpu.make_async_copy(
            amp_ref.at[i // 2, pl.ds((i % 2) * KB, KB), :],
            amp.at[pl.ds(pl.multiple_of(where_ref[1 + i], KB), KB), :],
            amp_sem.at[i],
        )
        for i in range(n_amp)
    ]

    def ints_copies(j):
        first = pl.multiple_of(j * 2 * KR + core * KR, KR)
        second = pl.multiple_of(j * 2 * KR + (1 - core) * KR, KR)
        return (
            pltpu.make_async_copy(mine_ref.at[j], ints.at[pl.ds(first, KR), :], ints_sem.at[0, j]),
            pltpu.make_async_copy(twin_ref.at[j], ints.at[pl.ds(second, KR), :], ints_sem.at[1, j]),
        )

    for copy in amp_copies:
        copy.start()
    for j in range(8):
        for copy in ints_copies(j):
            copy.start()
    for copy in amp_copies:
        copy.wait()
    out_ref[...] = jnp.zeros_like(out_ref)

    def step(s, carry):
        for j in range(2):
            for copy in ints_copies(s * 2 + j):
                copy.wait()
        rows = pl.ds(pl.multiple_of(s * 4 * KR, 4 * KR), 4 * KR)
        a_hi, a_lo = split(amp[rows, :].T)
        b_hi, b_lo = split(ints[rows, :])
        dot = lambda a, b: jnp.dot(a, b, preferred_element_type=F32)
        out_ref[...] += dot(a_hi, b_hi) + (dot(a_hi, b_lo) + dot(a_lo, b_hi))
        return carry

    lax.fori_loop(0, 4, step, 0)


def vmem(n):
    return [pl.BlockSpec(memory_space=pltpu.VMEM)] * n


def swap(v, axis):
    return lax.ppermute(v, axis, [(0, 1), (1, 0)])


def local(amp_packed, pair_rows, integrals):
    core, y_lo, z = lax.axis_index("core"), lax.axis_index("y_lo"), lax.axis_index("z")
    own = amp_packed.T
    other = swap(own, "y_lo")
    outgoing = pl.pallas_call(
        pack_kernel,
        out_shape=jax.ShapeDtypeStruct((ROWS, 256), F32),
        in_specs=vmem(3),
        out_specs=vmem(1)[0],
    )(pair_rows.reshape(1, ROWS), own, other)
    arrived = lax.all_to_all(outgoing, ("y_hi", "x", "core"), split_axis=0, concat_axis=0, tiled=True)
    mine = pl.pallas_call(
        unpack_kernel,
        out_shape=jax.ShapeDtypeStruct((2 * KB, ROWS), F32),
        in_specs=vmem(1),
        out_specs=vmem(1)[0],
    )(arrived)
    amp = lax.all_gather(mine, "z", axis=0, tiled=False)

    integrals, _ = lax.optimization_barrier((integrals, arrived))
    spread = jnp.broadcast_to(integrals[None], (8, KR, COLS))
    own_core = lax.all_to_all(spread, ("y_hi", "x"), split_axis=0, concat_axis=0, tiled=True)
    twin_core = swap(own_core, "core")

    zs = jnp.arange(16, dtype=jnp.int32)[:, None]
    halves = jnp.stack([y_lo, 1 - y_lo])[None, :]
    where = jnp.concatenate([core[None], (KB * (halves * 16 + zs)).reshape(-1)]).astype(jnp.int32)
    return pl.pallas_call(
        multiply_kernel,
        out_shape=jax.ShapeDtypeStruct((ROWS, COLS), F32),
        in_specs=[pl.BlockSpec(memory_space=pltpu.SMEM)] + [pl.BlockSpec(memory_space=pl.ANY)] * 3,
        out_specs=vmem(1)[0],
        scratch_shapes=[
            pltpu.VMEM((CD, ROWS), F32),
            pltpu.VMEM((CD, COLS), F32),
            pltpu.SemaphoreType.DMA((32,)),
            pltpu.SemaphoreType.DMA((2, 8)),
        ],
        compiler_params=pltpu.CompilerParams(vmem_limit_bytes=48 * 2**20),
        cost_estimate=pl.CostEstimate(flops=6 * ROWS * COLS * CD, bytes_accessed=15 * 2**20, transcendentals=0),
    )(where, amp, own_core, twin_core)


def solution(mesh):
    fine = Mesh(mesh.devices.reshape(2, 4, 2, 2, 16), ("y_hi", "x", "core", "y_lo", "z"))
    both = P(("y_hi", "x", "core"), ("y_lo", "z"))
    in_specs = (both, P(("y_hi", "x", "core")), both)
    return jax.shard_map(local, mesh=fine, in_specs=in_specs, out_specs=both, check_vma=False)
```

time: 297 us -> 144 us (0.48)
  the two profiles are of different devices: /device:TPU:1 before, /device:TPU:4 now
where the time goes in v1:
time: 144 us
  blocking collectives  78.1 us (54%)
  Pallas kernels  21.4 us (15%)
  waiting for transfers between devices  19.3 us (13%)
  between operations  13.4 us (9%)
  local copies, waits for them, and re-layouts  5.8 us (4%)
  starting transfers between devices  5.39 us (4%)
    all_to_all x1, blocking collectives, local(): lax.all_to_all(spread, ('y_hi', 'x'), split_axis=0, concat_axis=0, tiled=...  61 us
    all_to_all x1, blocking collectives, local(): lax.all_to_all(outgoing, ('y_hi', 'x', 'core'), split_axis=0, concat_axis...  17 us
    pallas_call x1, Pallas kernels, local(): pl.pallas_call(multiply_kernel, out_shape=jax.ShapeDtypeStruct((ROWS, COL...  16.5 us
    all_gather x1, waiting for transfers between devices, local(): amp = lax.all_gather(mine, 'z', axis=0, tiled=False)  16.4 us
    ppermute x2, starting transfers between devices, swap(): return lax.ppermute(v, axis, [(0, 1), (1, 0)])  5.38 us
    unnamed x4, local copies, waits for them, and re-layouts  2.99 us
    ppermute x2, waiting for transfers between devices, swap(): return lax.ppermute(v, axis, [(0, 1), (1, 0)])  2.95 us
  transfers between devices with their start and end apart: 3, of which 2 were waited for; matrix products, arithmetic and copies ran while one was open for 2% of the time, Pallas kernels for 0%

profile of v1, /device:TPU:4, one launch (start us, length us, event | category | flops | bytes accessed | tf_op | source)
XLA Modules:
  0.0 143.6 jit_solution(6819282497905752615)
XLA Ops:
  6.5 0.0 all-gather.3.cloned.1.call-start
  6.5 3.5 %collective-permute-start = (f32[96,384]{1,0:T(8,128)}, f32[96,384]{1,0:T(8,128)S(1)}, u32[]{:S(2)}, u32[]{:S(2)}) collective-permute-start(f32[96,384]{1,0:T(8,128)} %bitcast.10), channel_id=1, source_target_pairs={{0,16},{16,0},{1,17},{17,1},{2,18},{18,2},{3,19},{19,3},{4,20},{20... | collective-permute-start | bytes 442376 | tf_op jit(solution)/shard_map/ppermute | solution.py:114
  10.0 1.3 reshape.30.rows_ref
  11.3 2.9 %collective-permute-done.other_ref = f32[96,384]{1,0:T(8,128)S(1)} collective-permute-done((f32[96,384]{1,0:T(8,128)}, f32[96,384]{1,0:T(8,128)S(1)}, u32[]{:S(2)}, u32[]{:S(2)}) %collective-permute-start) | collective-permute-done | bytes 147488 | tf_op jit(solution)/shard_map/ppermute | solution.py:114
  14.2 0.0 copy-start.1
  14.2 0.7 copy-done.1
  14.9 2.5 %shard_map.37 = f32[384,256]{1,0:T(8,128)} custom-call(s32[1,384]{1,0:T(1,128)} %reshape.30.rows_ref, f32[96,384]{1,0:T(8,128)} %bitcast.11, f32[96,384]{1,0:T(8,128)} %copy-done.1), custom_call_target="tpu_custom_call" | custom-call | tf_op jit(solution)/shard_map/pallas_call | solution.py:121
  17.4 17.0 %all_to_all.16 = f32[16,24,256]{2,1,0:T(8,128)} all-to-all(f32[16,24,256]{2,1,0:T(8,128)} %bitcast.8), channel_id=1, replica_groups=mesh['y_hi'=2,'x'=4,'core'=2,'y_lo'=2,'z'=16] {'y_hi','x','core'}, dimensions={0} | all-to-all | bytes 786432 | tf_op jit(solution)/shard_map/all_to_all | solution.py:127
  34.4 2.4 %shard_map.38 = f32[192,384]{1,0:T(8,128)} custom-call(f32[384,256]{1,0:T(8,128)} %bitcast.9), custom_call_target="tpu_custom_call" | custom-call | tf_op jit(solution)/shard_map/pallas_call | solution.py:128
  36.8 0.0 all-gather.3.cloned.1.call-update
  36.8 1.5 %broadcast_in_dim.5 = f32[8,192,768]{2,1,0:T(8,128)S(1)} broadcast(f32[192,768]{1,0:T(8,128)} %param.5), dimensions={1,2} | broadcast | bytes 5308416 | tf_op jit(solution)/shard_map/broadcast_in_dim | solution.py:137
  38.3 61.0 %all_to_all.17.mine_ref = f32[8,192,768]{2,1,0:T(8,128)} all-to-all(f32[8,192,768]{2,1,0:T(8,128)S(1)} %broadcast_in_dim.5), channel_id=1, replica_groups=mesh['y_hi'=2,'x'=4,'core'=2,'y_lo'=2,'z'=16] {'y_hi','x'}, dimensions={0} | all-to-all | bytes 9437184 | tf_op jit(solution)/shard_map/all_to_all | solution.py:138
  99.3 1.9 %collective-permute-start.1 = (f32[8,192,768]{2,1,0:T(8,128)}, f32[8,192,768]{2,1,0:T(8,128)}, u32[]{:S(2)}, u32[]{:S(2)}) collective-permute-start(f32[8,192,768]{2,1,0:T(8,128)} %all_to_all.17.mine_ref), channel_id=1, source_target_pairs={{0,32},{32,0},{1,33},{33,1},{2,34},{34,2},{3,35},{35,3},{4,36},{36... | collective-permute-start | bytes 14155784 | tf_op jit(solution)/shard_map/ppermute | solution.py:114
  101.2 0.1 add_multiply_fusion.1
  101.3 0.1 mul.21
  101.4 0.1 pad_add_fusion.where_ref
  101.5 16.4 %all-gather.3.cloned.1.call-done = f32[3072,384]{1,0:T(8,128)} async-done(((f32[192,384]{1,0:T(8,128)}), f32[3072,384]{1,0:T(8,128)}) %all-gather.3.cloned.1.call-update) | async-done | bytes 4718608 | tf_op jit(solution)/shard_map/all_gather | solution.py:134
  117.9 0.0 collective-permute-done.1.twin_ref
  117.9 0.0 copy-start
  117.9 2.3 %copy-done = f32[3072,384]{1,0:T(8,128)S(1)} copy-done((f32[3072,384]{1,0:T(8,128)S(1)}, f32[3072,384]{1,0:T(8,128)}, u32[]{:S(2)}) %copy-start) | copy-done | bytes 4718616
  120.2 16.5 %shard_map.39 = f32[384,768]{1,0:T(8,128)} custom-call(s32[33]{0:T(128)S(1)} %pad_add_fusion.where_ref, f32[16,192,384]{2,1,0:T(8,128)S(1)} %bitcast.7, f32[8,192,768]{2,1,0:T(8,128)} %all_to_all.17.mine_ref, f32[8,192,768]{2,1,0:T(8,128)} %collective-permute-done.1.twin_ref), custom_call_target="tpu_custom_call" | custom-call | flops 5435817984 | bytes 15728640 | tf_op jit(solution)/shard_map/pallas_call | solution.py:144
  (1 shorter events, 0.0 us)
Async XLA Ops:
  6.5 111.3 %all-gather.3.cloned.1.call-start = ((), (), s32[]{:S(2)}) async-start(), calls=%async_computation.2 | async-start | bytes 5013504 | tf_op jit(solution)/shard_map/all_gather | solution.py:134
  6.5 7.7 %collective-permute-start = (f32[96,384]{1,0:T(8,128)}, f32[96,384]{1,0:T(8,128)S(1)}, u32[]{:S(2)}, u32[]{:S(2)}) collective-permute-start(f32[96,384]{1,0:T(8,128)} %bitcast.10), channel_id=1, source_target_pairs={{0,16},{16,0},{1,17},{17,1},{2,18},{18,2},{3,19},{19,3},{4,20},{20... | collective-permute-start | bytes 442376 | tf_op jit(solution)/shard_map/ppermute | solution.py:114
  14.2 0.7 copy-start.1
  99.3 18.6 %collective-permute-start.1 = (f32[8,192,768]{2,1,0:T(8,128)}, f32[8,192,768]{2,1,0:T(8,128)}, u32[]{:S(2)}, u32[]{:S(2)}) collective-permute-start(f32[8,192,768]{2,1,0:T(8,128)} %all_to_all.17.mine_ref), channel_id=1, source_target_pairs={{0,32},{32,0},{1,33},{33,1},{2,34},{34,2},{3,35},{35,3},{4,36},{36... | collective-permute-start | bytes 14155784 | tf_op jit(solution)/shard_map/ppermute | solution.py:114
  117.9 2.3 %copy-start = (f32[3072,384]{1,0:T(8,128)S(1)}, f32[3072,384]{1,0:T(8,128)}, u32[]{:S(2)}) copy-start(f32[3072,384]{1,0:T(8,128)} %all-gather.3.cloned.1.call-done) | copy-start | bytes 14155780
Sparse Core Ops, SparseCore 0:
  37.0 80.8 all-gather.2

commit v2 on v1

v2 whole, which is shorter than its diff:
```python
import jax
import jax.numpy as jnp
from jax import lax
from jax.experimental import pallas as pl
from jax.experimental.pallas import tpu as pltpu
from jax.sharding import Mesh, PartitionSpec as P

F32 = jnp.float32
BF16 = jnp.bfloat16
ROWS = 384
KB = 96
COLS = 768
KR = 192
CD = 3072
SEND = 24


def exact_pick(onehot, values):
    hi = values.astype(BF16)
    rest = values - hi.astype(F32)
    mid = rest.astype(BF16)
    lo = (rest - mid.astype(F32)).astype(BF16)
    dot = lambda part: jnp.dot(onehot, part, preferred_element_type=F32)
    return (dot(hi) + dot(mid)) + dot(lo)


def pack_kernel(rows_ref, amp_ref, out_ref):
    rows = rows_ref[...].reshape(1, ROWS)
    block = ((rows >> 7) * 171) >> 9
    place = rows - block * ROWS
    down = lax.broadcasted_iota(jnp.int32, (ROWS, ROWS), 0)
    along = lax.broadcasted_iota(jnp.int32, (ROWS, ROWS), 1)
    block_f = block.astype(F32)
    diagonal = down == along
    column = lambda v: jnp.sum(jnp.where(diagonal, v, 0.0), axis=1, keepdims=True)
    same = (column(block_f) == block_f) & (down < along)
    rank = jnp.sum(jnp.where(same, 1.0, 0.0), axis=0, keepdims=True)
    position = block_f * float(SEND) + rank
    onehot = jnp.where(down.astype(F32) == position, 1.0, 0.0).astype(BF16)
    places = jnp.broadcast_to(column(place.astype(F32)), (ROWS, 128 - KB))
    values = jnp.concatenate([amp_ref[...].T, places], axis=1)
    packed = exact_pick(onehot, values)
    out_ref[:ROWS, :] = packed
    out_ref[ROWS:, :] = packed


def unpack_kernel(arrived_ref, out_ref):
    places = arrived_ref[:ROWS, KB : KB + 1]
    along = lax.broadcasted_iota(jnp.int32, (ROWS, ROWS), 1).astype(F32)
    onehot = jnp.where(along == places, 1.0, 0.0).astype(BF16)
    flipped = jnp.concatenate([arrived_ref[:ROWS, :].T[:KB], arrived_ref[ROWS:, :].T[:KB]])
    hi = flipped.astype(BF16)
    rest = flipped - hi.astype(F32)
    mid = rest.astype(BF16)
    lo = (rest - mid.astype(F32)).astype(BF16)
    dot = lambda part: jnp.dot(part, onehot, preferred_element_type=F32)
    out_ref[...] = (dot(hi) + dot(mid)) + dot(lo)


def split(v):
    hi = v.astype(BF16)
    return hi, (v - hi.astype(F32)).astype(BF16)


def multiply_kernel(core_ref, amp_ref, *refs):
    ints_refs, (out_ref, amp, amp_hi, amp_lo, sem) = refs[:2], refs[2:]
    core = core_ref[0]

    def amp_copies(i):
        which = core if i < 2 else 1 - core
        return [
            pltpu.make_async_copy(
                amp_ref.at[pl.ds(4 * j + 2 * which, 2), pl.ds(i % 2 * KB, KB), :],
                amp.at[pl.ds(8 * i + 2 * j, 2)],
                sem.at[i, j],
            )
            for j in range(4)
        ]

    for i in range(4):
        for copy in amp_copies(i):
            copy.start()
    for i in range(4):
        for copy in amp_copies(i):
            copy.wait()
        columns = slice(i * 4 * KR, (i + 1) * 4 * KR)
        amp_hi[:, columns], amp_lo[:, columns] = split(amp[8 * i : 8 * i + 8].reshape(4 * KR, ROWS).T)
    dot = lambda a, b: jnp.dot(a, b, preferred_element_type=F32)
    half = CD // 2
    for i in range(2):
        b_hi, b_lo = split(ints_refs[i][...])
        a_hi, a_lo = (ref[:, i * half : (i + 1) * half] for ref in (amp_hi, amp_lo))
        part = dot(a_hi, b_hi) + (dot(a_hi, b_lo) + dot(a_lo, b_hi))
        out_ref[...] = part if i == 0 else out_ref[...] + part


def vmem(n):
    return [pl.BlockSpec(memory_space=pltpu.VMEM)] * n


def swap(v, axis):
    return lax.ppermute(v, axis, [(0, 1), (1, 0)])


def local(amp_packed, pair_rows, integrals):
    outgoing = pl.pallas_call(
        pack_kernel,
        out_shape=jax.ShapeDtypeStruct((2 * ROWS, 128), F32),
        in_specs=vmem(2),
        out_specs=vmem(1)[0],
    )(pair_rows, amp_packed.T)
    arrived = lax.all_to_all(outgoing, ("y_lo", "y_hi", "x", "core"), split_axis=0, concat_axis=0, tiled=True)
    mine = pl.pallas_call(
        unpack_kernel,
        out_shape=jax.ShapeDtypeStruct((2 * KB, ROWS), F32),
        in_specs=vmem(1),
        out_specs=vmem(1)[0],
    )(arrived)
    amp = lax.all_gather(mine, "z", axis=0, tiled=False)

    integrals, _ = lax.optimization_barrier((integrals, arrived))
    spread = jnp.broadcast_to(integrals[None], (8, KR, COLS))
    gathered = lax.all_to_all(spread, ("y_hi", "x"), split_axis=0, concat_axis=0, tiled=True)
    twin = swap(gathered, "core")

    return pl.pallas_call(
        multiply_kernel,
        out_shape=jax.ShapeDtypeStruct((ROWS, COLS), F32),
        in_specs=[pl.BlockSpec(memory_space=pltpu.SMEM)] + [pl.BlockSpec(memory_space=pl.ANY)] + vmem(2),
        out_specs=vmem(1)[0],
        scratch_shapes=[
            pltpu.VMEM((32, KB, ROWS), F32),
            pltpu.VMEM((ROWS, CD), BF16),
            pltpu.VMEM((ROWS, CD), BF16),
            pltpu.SemaphoreType.DMA((4, 4)),
        ],
        compiler_params=pltpu.CompilerParams(vmem_limit_bytes=48 * 2**20),
        cost_estimate=pl.CostEstimate(flops=6 * ROWS * COLS * CD, bytes_accessed=15 * 2**20, transcendentals=0),
    )(lax.axis_index("core")[None], amp, gathered.reshape(CD // 2, COLS), twin.reshape(CD // 2, COLS))


def solution(mesh):
    fine = Mesh(mesh.devices.reshape(2, 4, 2, 2, 16), ("y_hi", "x", "core", "y_lo", "z"))
    both = P(("y_hi", "x", "core"), ("y_lo", "z"))
    in_specs = (both, P(("y_hi", "x", "core")), both)
    return jax.shard_map(local, mesh=fine, in_specs=in_specs, out_specs=both, check_vma=False)
```

time: 144 us -> 132 us (0.917)
  Pallas kernels: 21.4 us -> 17 us
  starting transfers between devices: 5.39 us -> 1.91 us
  waiting for transfers between devices: 19.3 us -> 16.7 us
  local copies, waits for them, and re-layouts: 5.8 us -> 3.8 us
    pallas_call x1, Pallas kernels: 16.5 us -> 12.3 us  [local(): pl.pallas_call(multiply_kernel, out_shape=jax.ShapeDtypeStruct((ROWS, COL...]
    ppermute x2 -> x1, starting transfers between devices: 5.38 us -> 1.91 us  [swap(): return lax.ppermute(v, axis, [(0, 1), (1, 0)])]
    ppermute x2 -> x1, waiting for transfers between devices: 2.95 us -> 0.01 us  [swap(): return lax.ppermute(v, axis, [(0, 1), (1, 0)])]
    unnamed x4 -> x2, local copies, waits for them, and re-layouts: 2.99 us -> 2.34 us
  transfers between devices with their start and end apart: 3 -> 2, of which waited for: 2 -> 1; matrix products, arithmetic and copies ran while one was open for 2% -> 1% of each run, Pallas kernels for 0% -> 0%
where the time goes in v2:
time: 132 us; the launch traced here: 131 us
  blocking collectives  78.7 us (60%)
  Pallas kernels  17 us (13%)
  waiting for transfers between devices  16.7 us (13%)
  between operations  13.4 us (10%)
  local copies, waits for them, and re-layouts  3.8 us (3%)
  starting transfers between devices  1.91 us (1%)
    all_to_all x1, blocking collectives, local(): lax.all_to_all(spread, ('y_hi', 'x'), split_axis=0, concat_axis=0, tiled=...  60.2 us
    all_to_all x1, blocking collectives, local(): lax.all_to_all(outgoing, ('y_lo', 'y_hi', 'x', 'core'), split_axis=0, con...  18.5 us
    all_gather x1, waiting for transfers between devices, local(): amp = lax.all_gather(mine, 'z', axis=0, tiled=False)  16.6 us
    pallas_call x1, Pallas kernels, local(): pl.pallas_call(multiply_kernel, out_shape=jax.ShapeDtypeStruct((ROWS, COL...  12.3 us
  transfers between devices with their start and end apart: 2, of which 1 were waited for; matrix products, arithmetic and copies ran while one was open for 1% of the time, Pallas kernels for 0%

profile of v2, /device:TPU:4, one launch (start us, length us, event | category | flops | bytes accessed | tf_op | source)
XLA Modules:
  0.0 131.5 jit_solution(5401161072875592935)
XLA Ops:
  6.5 0.0 all-gather.3.cloned.1.call-start
  6.5 2.3 %shard_map.37 = f32[768,128]{1,0:T(8,128)} custom-call(s32[384]{0:T(512)} %rows_ref.1, f32[96,384]{1,0:T(8,128)} %bitcast.10), custom_call_target="tpu_custom_call" | custom-call | tf_op jit(solution)/shard_map/pallas_call | solution.py:106
  8.9 18.5 %all_to_all.16 = f32[32,24,128]{2,1,0:T(8,128)} all-to-all(f32[32,24,128]{2,1,0:T(8,128)} %bitcast.8), channel_id=1, replica_groups=mesh['y_hi'=2,'x'=4,'core'=2,'y_lo'=2,'z'=16] {'y_lo','y_hi','x','core'}, dimensions={0} | all-to-all | bytes 786432 | tf_op jit(solution)/shard_map/all_to_all | solution.py:112
  27.3 2.3 %shard_map.38 = f32[192,384]{1,0:T(8,128)} custom-call(f32[768,128]{1,0:T(8,128)} %bitcast.9), custom_call_target="tpu_custom_call" | custom-call | tf_op jit(solution)/shard_map/pallas_call | solution.py:113
  29.7 0.0 all-gather.3.cloned.1.call-update
  29.7 1.5 %broadcast_in_dim.10 = f32[8,192,768]{2,1,0:T(8,128)S(1)} broadcast(f32[192,768]{1,0:T(8,128)} %param.5), dimensions={1,2} | broadcast | bytes 5308416 | tf_op jit(solution)/shard_map/broadcast_in_dim | solution.py:122
  31.2 60.2 %all_to_all.17 = f32[8,192,768]{2,1,0:T(8,128)} all-to-all(f32[8,192,768]{2,1,0:T(8,128)S(1)} %broadcast_in_dim.10), channel_id=1, replica_groups=mesh['y_hi'=2,'x'=4,'core'=2,'y_lo'=2,'z'=16] {'y_hi','x'}, dimensions={0} | all-to-all | bytes 9437184 | tf_op jit(solution)/shard_map/all_to_all | solution.py:123
  91.4 1.9 %collective-permute-start = (f32[8,192,768]{2,1,0:T(8,128)}, f32[8,192,768]{2,1,0:T(8,128)}, u32[]{:S(2)}, u32[]{:S(2)}) collective-permute-start(f32[8,192,768]{2,1,0:T(8,128)} %all_to_all.17), channel_id=1, source_target_pairs={{0,32},{32,0},{1,33},{33,1},{2,34},{34,2},{3,35},{35,3},{4,36},{36... | collective-permute-start | bytes 14155784 | tf_op jit(solution)/shard_map/ppermute | solution.py:102
  93.3 16.6 %all-gather.3.cloned.1.call-done = f32[3072,384]{1,0:T(8,128)} async-done(((f32[192,384]{1,0:T(8,128)}), f32[3072,384]{1,0:T(8,128)}) %all-gather.3.cloned.1.call-update) | async-done | bytes 4718608 | tf_op jit(solution)/shard_map/all_gather | solution.py:119
  109.9 0.0 collective-permute-done
  109.9 0.0 copy-start
  109.9 2.3 %copy-done = f32[3072,384]{1,0:T(8,128)S(1)} copy-done((f32[3072,384]{1,0:T(8,128)S(1)}, f32[3072,384]{1,0:T(8,128)}, u32[]{:S(2)}) %copy-start) | copy-done | bytes 4718616
  112.3 12.3 %shard_map.39 = f32[384,768]{1,0:T(8,128)} custom-call(s32[1]{0:T(128)} %bitcast.core_ref, f32[16,192,384]{2,1,0:T(8,128)S(1)} %bitcast.7, f32[1536,768]{1,0:T(8,128)} %bitcast.5.refs_0_, f32[1536,768]{1,0:T(8,128)} %bitcast.6.refs_1_), custom_call_target="tpu_custom_call" | custom-call | flops 5435817984 | bytes 15728640 | tf_op jit(solution)/shard_map/pallas_call | solution.py:126
Async XLA Ops:
  6.5 103.4 %all-gather.3.cloned.1.call-start = ((), (), s32[]{:S(2)}) async-start(), calls=%async_computation.2 | async-start | bytes 5013504 | tf_op jit(solution)/shard_map/all_gather | solution.py:119
  91.4 18.6 %collective-permute-start = (f32[8,192,768]{2,1,0:T(8,128)}, f32[8,192,768]{2,1,0:T(8,128)}, u32[]{:S(2)}, u32[]{:S(2)}) collective-permute-start(f32[8,192,768]{2,1,0:T(8,128)} %all_to_all.17), channel_id=1, source_target_pairs={{0,32},{32,0},{1,33},{33,1},{2,34},{34,2},{3,35},{35,3},{4,36},{36... | collective-permute-start | bytes 14155784 | tf_op jit(solution)/shard_map/ppermute | solution.py:102
  109.9 2.3 %copy-start = (f32[3072,384]{1,0:T(8,128)S(1)}, f32[3072,384]{1,0:T(8,128)}, u32[]{:S(2)}) copy-start(f32[3072,384]{1,0:T(8,128)} %all-gather.3.cloned.1.call-done) | copy-start | bytes 14155780
Sparse Core Ops, SparseCore 0:
  29.8 80.0 all-gather.2

commit v3 on v2

--- a/solution.py
+++ b/solution.py
@@ -63,7 +63,7 @@
 
 
 def multiply_kernel(core_ref, amp_ref, *refs):
-    ints_refs, (out_ref, amp, amp_hi, amp_lo, sem) = refs[:2], refs[2:]
+    ints_refs, (out_ref, amp, amp_hi, amp_lo, ints, ints_hi, ints_lo, sem, ints_sem) = refs[:2], refs[2:]
     core = core_ref[0]
 
     def amp_copies(i):
@@ -77,21 +77,28 @@
             for j in range(4)
         ]
 
+    def ints_copy(i):
+        rows = pl.ds(i % 2 * 4 * KR, 4 * KR)
+        return pltpu.make_async_copy(ints_refs[i // 2].at[rows, :], ints.at[i], ints_sem.at[i])
+
+    for i in (0, 2):
+        for copy in amp_copies(i) + amp_copies(i + 1) + [ints_copy(i), ints_copy(i + 1)]:
+            copy.start()
+    dot = lambda a, b: jnp.dot(a, b, preferred_element_type=F32)
     for i in range(4):
-        for copy in amp_copies(i):
-            copy.start()
-    for i in range(4):
+        here = slice(i * 4 * KR, (i + 1) * 4 * KR)
         for copy in amp_copies(i):
             copy.wait()
-        columns = slice(i * 4 * KR, (i + 1) * 4 * KR)
-        amp_hi[:, columns], amp_lo[:, columns] = split(amp[8 * i : 8 * i + 8].reshape(4 * KR, ROWS).T)
-    dot = lambda a, b: jnp.dot(a, b, preferred_element_type=F32)
-    half = CD // 2
-    for i in range(2):
-        b_hi, b_lo = split(ints_refs[i][...])
-        a_hi, a_lo = (ref[:, i * half : (i + 1) * half] for ref in (amp_hi, amp_lo))
-        part = dot(a_hi, b_hi) + (dot(a_hi, b_lo) + dot(a_lo, b_hi))
-        out_ref[...] = part if i == 0 else out_ref[...] + part
+        amp_hi[:, here], amp_lo[:, here] = split(amp[8 * i : 8 * i + 8].reshape(4 * KR, ROWS).T)
+        if i % 2 == 1:
+            for k in (i - 1, i):
+                ints_copy(k).wait()
+                rows = slice(k * 4 * KR, (k + 1) * 4 * KR)
+                ints_hi[rows, :], ints_lo[rows, :] = split(ints[k])
+            here = slice((i - 1) * 4 * KR, (i + 1) * 4 * KR)
+            a_hi, a_lo, b_hi, b_lo = amp_hi[:, here], amp_lo[:, here], ints_hi[here, :], ints_lo[here, :]
+            part = dot(a_hi, b_hi) + (dot(a_hi, b_lo) + dot(a_lo, b_hi))
+            out_ref[...] = part if i == 1 else out_ref[...] + part
 
 
 def vmem(n):
@@ -126,15 +133,19 @@
     return pl.pallas_call(
         multiply_kernel,
         out_shape=jax.ShapeDtypeStruct((ROWS, COLS), F32),
-        in_specs=[pl.BlockSpec(memory_space=pltpu.SMEM)] + [pl.BlockSpec(memory_space=pl.ANY)] + vmem(2),
+        in_specs=[pl.BlockSpec(memory_space=pltpu.SMEM)] + [pl.BlockSpec(memory_space=pl.ANY)] * 3,
         out_specs=vmem(1)[0],
         scratch_shapes=[
             pltpu.VMEM((32, KB, ROWS), F32),
             pltpu.VMEM((ROWS, CD), BF16),
             pltpu.VMEM((ROWS, CD), BF16),
+            pltpu.VMEM((4, 4 * KR, COLS), F32),
+            pltpu.VMEM((CD, COLS), BF16),
+            pltpu.VMEM((CD, COLS), BF16),
             pltpu.SemaphoreType.DMA((4, 4)),
+            pltpu.SemaphoreType.DMA((4,)),
         ],
-        compiler_params=pltpu.CompilerParams(vmem_limit_bytes=48 * 2**20),
+        compiler_params=pltpu.CompilerParams(vmem_limit_bytes=60 * 2**20),
         cost_estimate=pl.CostEstimate(flops=6 * ROWS * COLS * CD, bytes_accessed=15 * 2**20, transcendentals=0),
     )(lax.axis_index("core")[None], amp, gathered.reshape(CD // 2, COLS), twin.reshape(CD // 2, COLS))
 

time: 132 us -> 131 us (level)
  local copies, waits for them, and re-layouts: 3.8 us -> 1.46 us
    unnamed x2 -> x0, local copies, waits for them, and re-layouts: 2.34 us -> none
where the time goes in v3:
time: 131 us; the launch traced here: 130 us
  blocking collectives  78.7 us (60%)
  Pallas kernels  18 us (14%)
  waiting for transfers between devices  16.7 us (13%)
  between operations  13.4 us (10%)
  starting transfers between devices  1.91 us (1%)
  local copies, waits for them, and re-layouts  1.46 us (1%)
    all_to_all x1, blocking collectives, local(): lax.all_to_all(spread, ('y_hi', 'x'), split_axis=0, concat_axis=0, tiled=...  60.2 us
    all_to_all x1, blocking collectives, local(): lax.all_to_all(outgoing, ('y_lo', 'y_hi', 'x', 'core'), split_axis=0, con...  18.5 us
    all_gather x1, waiting for transfers between devices, local(): amp = lax.all_gather(mine, 'z', axis=0, tiled=False)  16.6 us
    pallas_call x1, Pallas kernels, local(): pl.pallas_call(multiply_kernel, out_shape=jax.ShapeDtypeStruct((ROWS, COL...  13.4 us
  transfers between devices with their start and end apart: 2, of which 1 were waited for; matrix products, arithmetic and copies ran while one was open for 1% of the time, Pallas kernels for 0%

profile of v3, /device:TPU:4, one launch (start us, length us, event | category | flops | bytes accessed | tf_op | source)
XLA Modules:
  0.0 130.2 jit_solution(3957683245031846376)
XLA Ops:
  6.5 0.0 all-gather.3.cloned.1.call-start
  6.5 2.3 %shard_map.37 = f32[768,128]{1,0:T(8,128)} custom-call(s32[384]{0:T(512)} %rows_ref.1, f32[96,384]{1,0:T(8,128)} %bitcast.9), custom_call_target="tpu_custom_call" | custom-call | tf_op jit(solution)/shard_map/pallas_call | solution.py:113
  8.9 18.5 %all_to_all.16 = f32[32,24,128]{2,1,0:T(8,128)} all-to-all(f32[32,24,128]{2,1,0:T(8,128)} %bitcast.7), channel_id=1, replica_groups=mesh['y_hi'=2,'x'=4,'core'=2,'y_lo'=2,'z'=16] {'y_lo','y_hi','x','core'}, dimensions={0} | all-to-all | bytes 786432 | tf_op jit(solution)/shard_map/all_to_all | solution.py:119
  27.3 2.3 %shard_map.38 = f32[192,384]{1,0:T(8,128)} custom-call(f32[768,128]{1,0:T(8,128)} %bitcast.8), custom_call_target="tpu_custom_call" | custom-call | tf_op jit(solution)/shard_map/pallas_call | solution.py:120
  29.7 0.0 all-gather.3.cloned.1.call-update
  29.7 1.5 %broadcast_in_dim.10 = f32[8,192,768]{2,1,0:T(8,128)S(1)} broadcast(f32[192,768]{1,0:T(8,128)} %param.5), dimensions={1,2} | broadcast | bytes 5308416 | tf_op jit(solution)/shard_map/broadcast_in_dim | solution.py:129
  31.2 60.2 %all_to_all.17 = f32[8,192,768]{2,1,0:T(8,128)} all-to-all(f32[8,192,768]{2,1,0:T(8,128)S(1)} %broadcast_in_dim.10), channel_id=1, replica_groups=mesh['y_hi'=2,'x'=4,'core'=2,'y_lo'=2,'z'=16] {'y_hi','x'}, dimensions={0} | all-to-all | bytes 9437184 | tf_op jit(solution)/shard_map/all_to_all | solution.py:130
  91.4 1.9 %collective-permute-start = (f32[8,192,768]{2,1,0:T(8,128)}, f32[8,192,768]{2,1,0:T(8,128)}, u32[]{:S(2)}, u32[]{:S(2)}) collective-permute-start(f32[8,192,768]{2,1,0:T(8,128)} %all_to_all.17), channel_id=1, source_target_pairs={{0,32},{32,0},{1,33},{33,1},{2,34},{34,2},{3,35},{35,3},{4,36},{36... | collective-permute-start | bytes 14155784 | tf_op jit(solution)/shard_map/ppermute | solution.py:109
  93.3 16.6 %all-gather.3.cloned.1.call-done = f32[3072,384]{1,0:T(8,128)} async-done(((f32[192,384]{1,0:T(8,128)}), f32[3072,384]{1,0:T(8,128)}) %all-gather.3.cloned.1.call-update) | async-done | bytes 4718608 | tf_op jit(solution)/shard_map/all_gather | solution.py:126
  109.9 0.0 collective-permute-done
  109.9 13.4 %shard_map.39 = f32[384,768]{1,0:T(8,128)} custom-call(s32[1]{0:T(128)} %bitcast.core_ref, f32[16,192,384]{2,1,0:T(8,128)} %bitcast.10, f32[1536,768]{1,0:T(8,128)} %bitcast.5.refs_0_, f32[1536,768]{1,0:T(8,128)} %bitcast.6.refs_1_), custom_call_target="tpu_custom_call" | custom-call | flops 5435817984 | bytes 15728640 | tf_op jit(solution)/shard_map/pallas_call | solution.py:133
Async XLA Ops:
  6.5 103.4 %all-gather.3.cloned.1.call-start = ((), (), s32[]{:S(2)}) async-start(), calls=%async_computation.2 | async-start | bytes 5013504 | tf_op jit(solution)/shard_map/all_gather | solution.py:126
  91.4 18.6 %collective-permute-start = (f32[8,192,768]{2,1,0:T(8,128)}, f32[8,192,768]{2,1,0:T(8,128)}, u32[]{:S(2)}, u32[]{:S(2)}) collective-permute-start(f32[8,192,768]{2,1,0:T(8,128)} %all_to_all.17), channel_id=1, source_target_pairs={{0,32},{32,0},{1,33},{33,1},{2,34},{34,2},{3,35},{35,3},{4,36},{36... | collective-permute-start | bytes 14155784 | tf_op jit(solution)/shard_map/ppermute | solution.py:109
Sparse Core Ops, SparseCore 0:
  29.8 80.0 all-gather.2

commit v4 on v3

--- a/solution.py
+++ b/solution.py
@@ -81,24 +81,18 @@
         rows = pl.ds(i % 2 * 4 * KR, 4 * KR)
         return pltpu.make_async_copy(ints_refs[i // 2].at[rows, :], ints.at[i], ints_sem.at[i])
 
-    for i in (0, 2):
-        for copy in amp_copies(i) + amp_copies(i + 1) + [ints_copy(i), ints_copy(i + 1)]:
+    for i in range(4):
+        for copy in [ints_copy(i)] + amp_copies(i):
             copy.start()
-    dot = lambda a, b: jnp.dot(a, b, preferred_element_type=F32)
     for i in range(4):
         here = slice(i * 4 * KR, (i + 1) * 4 * KR)
         for copy in amp_copies(i):
             copy.wait()
-        amp_hi[:, here], amp_lo[:, here] = split(amp[8 * i : 8 * i + 8].reshape(4 * KR, ROWS).T)
-        if i % 2 == 1:
-            for k in (i - 1, i):
-                ints_copy(k).wait()
-                rows = slice(k * 4 * KR, (k + 1) * 4 * KR)
-                ints_hi[rows, :], ints_lo[rows, :] = split(ints[k])
-            here = slice((i - 1) * 4 * KR, (i + 1) * 4 * KR)
-            a_hi, a_lo, b_hi, b_lo = amp_hi[:, here], amp_lo[:, here], ints_hi[here, :], ints_lo[here, :]
-            part = dot(a_hi, b_hi) + (dot(a_hi, b_lo) + dot(a_lo, b_hi))
-            out_ref[...] = part if i == 1 else out_ref[...] + part
+        amp_hi[here, :], amp_lo[here, :] = split(amp[8 * i : 8 * i + 8].reshape(4 * KR, ROWS))
+        ints_copy(i).wait()
+        ints_hi[here, :], ints_lo[here, :] = split(ints[i])
+    dot = lambda a, b: lax.dot_general(a[...], b[...], (((0,), (0,)), ((), ())), preferred_element_type=F32)
+    out_ref[...] = dot(amp_hi, ints_hi) + (dot(amp_hi, ints_lo) + dot(amp_lo, ints_hi))
 
 
 def vmem(n):
@@ -137,8 +131,8 @@
         out_specs=vmem(1)[0],
         scratch_shapes=[
             pltpu.VMEM((32, KB, ROWS), F32),
-            pltpu.VMEM((ROWS, CD), BF16),
-            pltpu.VMEM((ROWS, CD), BF16),
+            pltpu.VMEM((CD, ROWS), BF16),
+            pltpu.VMEM((CD, ROWS), BF16),
             pltpu.VMEM((4, 4 * KR, COLS), F32),
             pltpu.VMEM((CD, COLS), BF16),
             pltpu.VMEM((CD, COLS), BF16),

time: 131 us -> 129 us (0.985)
    pallas_call x1, Pallas kernels: 13.4 us -> 12 us  [local(): pl.pallas_call(multiply_kernel, out_shape=jax.ShapeDtypeStruct((ROWS, COL...]
where the time goes in v4:
time: 129 us
  blocking collectives  78.7 us (61%)
  Pallas kernels  16.7 us (13%)
  waiting for transfers between devices  16.7 us (13%)
  between operations  13.4 us (10%)
  starting transfers between devices  1.91 us (1%)
  local copies, waits for them, and re-layouts  1.46 us (1%)
    all_to_all x1, blocking collectives, local(): lax.all_to_all(spread, ('y_hi', 'x'), split_axis=0, concat_axis=0, tiled=...  60.2 us
    all_to_all x1, blocking collectives, local(): lax.all_to_all(outgoing, ('y_lo', 'y_hi', 'x', 'core'), split_axis=0, con...  18.5 us
    all_gather x1, waiting for transfers between devices, local(): amp = lax.all_gather(mine, 'z', axis=0, tiled=False)  16.6 us
    pallas_call x1, Pallas kernels, local(): pl.pallas_call(multiply_kernel, out_shape=jax.ShapeDtypeStruct((ROWS, COL...  12 us
  transfers between devices with their start and end apart: 2, of which 1 were waited for; matrix products, arithmetic and copies ran while one was open for 1% of the time, Pallas kernels for 0%

profile of v4, /device:TPU:4, one launch (start us, length us, event | category | flops | bytes accessed | tf_op | source)
XLA Modules:
  0.0 128.8 jit_solution(15630367263375060644)
XLA Ops:
  6.5 0.0 all-gather.3.cloned.1.call-start
  6.5 2.3 %shard_map.37 = f32[768,128]{1,0:T(8,128)} custom-call(s32[384]{0:T(512)} %rows_ref.1, f32[96,384]{1,0:T(8,128)} %bitcast.9), custom_call_target="tpu_custom_call" | custom-call | tf_op jit(solution)/shard_map/pallas_call | solution.py:107
  8.9 18.5 %all_to_all.16 = f32[32,24,128]{2,1,0:T(8,128)} all-to-all(f32[32,24,128]{2,1,0:T(8,128)} %bitcast.7), channel_id=1, replica_groups=mesh['y_hi'=2,'x'=4,'core'=2,'y_lo'=2,'z'=16] {'y_lo','y_hi','x','core'}, dimensions={0} | all-to-all | bytes 786432 | tf_op jit(solution)/shard_map/all_to_all | solution.py:113
  27.3 2.3 %shard_map.38 = f32[192,384]{1,0:T(8,128)} custom-call(f32[768,128]{1,0:T(8,128)} %bitcast.8), custom_call_target="tpu_custom_call" | custom-call | tf_op jit(solution)/shard_map/pallas_call | solution.py:114
  29.7 0.0 all-gather.3.cloned.1.call-update
  29.7 1.5 %broadcast_in_dim.10 = f32[8,192,768]{2,1,0:T(8,128)S(1)} broadcast(f32[192,768]{1,0:T(8,128)} %param.5), dimensions={1,2} | broadcast | bytes 5308416 | tf_op jit(solution)/shard_map/broadcast_in_dim | solution.py:123
  31.2 60.2 %all_to_all.17 = f32[8,192,768]{2,1,0:T(8,128)} all-to-all(f32[8,192,768]{2,1,0:T(8,128)S(1)} %broadcast_in_dim.10), channel_id=1, replica_groups=mesh['y_hi'=2,'x'=4,'core'=2,'y_lo'=2,'z'=16] {'y_hi','x'}, dimensions={0} | all-to-all | bytes 9437184 | tf_op jit(solution)/shard_map/all_to_all | solution.py:124
  91.4 1.9 %collective-permute-start = (f32[8,192,768]{2,1,0:T(8,128)}, f32[8,192,768]{2,1,0:T(8,128)}, u32[]{:S(2)}, u32[]{:S(2)}) collective-permute-start(f32[8,192,768]{2,1,0:T(8,128)} %all_to_all.17), channel_id=1, source_target_pairs={{0,32},{32,0},{1,33},{33,1},{2,34},{34,2},{3,35},{35,3},{4,36},{36... | collective-permute-start | bytes 14155784 | tf_op jit(solution)/shard_map/ppermute | solution.py:103
  93.3 16.6 %all-gather.3.cloned.1.call-done = f32[3072,384]{1,0:T(8,128)} async-done(((f32[192,384]{1,0:T(8,128)}), f32[3072,384]{1,0:T(8,128)}) %all-gather.3.cloned.1.call-update) | async-done | bytes 4718608 | tf_op jit(solution)/shard_map/all_gather | solution.py:120
  109.9 0.0 collective-permute-done
  109.9 12.0 %shard_map.39 = f32[384,768]{1,0:T(8,128)} custom-call(s32[1]{0:T(128)} %bitcast.core_ref, f32[16,192,384]{2,1,0:T(8,128)} %bitcast.10, f32[1536,768]{1,0:T(8,128)} %bitcast.5.refs_0_, f32[1536,768]{1,0:T(8,128)} %bitcast.6.refs_1_), custom_call_target="tpu_custom_call" | custom-call | flops 5435817984 | bytes 15728640 | tf_op jit(solution)/shard_map/pallas_call | solution.py:127
Async XLA Ops:
  6.5 103.4 %all-gather.3.cloned.1.call-start = ((), (), s32[]{:S(2)}) async-start(), calls=%async_computation.2 | async-start | bytes 5013504 | tf_op jit(solution)/shard_map/all_gather | solution.py:120
  91.4 18.6 %collective-permute-start = (f32[8,192,768]{2,1,0:T(8,128)}, f32[8,192,768]{2,1,0:T(8,128)}, u32[]{:S(2)}, u32[]{:S(2)}) collective-permute-start(f32[8,192,768]{2,1,0:T(8,128)} %all_to_all.17), channel_id=1, source_target_pairs={{0,32},{32,0},{1,33},{33,1},{2,34},{34,2},{3,35},{35,3},{4,36},{36... | collective-permute-start | bytes 14155784 | tf_op jit(solution)/shard_map/ppermute | solution.py:103
Sparse Core Ops, SparseCore 0:
  29.8 80.0 all-gather.2

commit v5 on v4

--- a/solution.py
+++ b/solution.py
@@ -15,12 +15,11 @@
 SEND = 24
 
 
-def exact_pick(onehot, values):
+def exact_dot(dot, values):
     hi = values.astype(BF16)
     rest = values - hi.astype(F32)
     mid = rest.astype(BF16)
     lo = (rest - mid.astype(F32)).astype(BF16)
-    dot = lambda part: jnp.dot(onehot, part, preferred_element_type=F32)
     return (dot(hi) + dot(mid)) + dot(lo)
 
 
@@ -37,9 +36,11 @@
     rank = jnp.sum(jnp.where(same, 1.0, 0.0), axis=0, keepdims=True)
     position = block_f * float(SEND) + rank
     onehot = jnp.where(down.astype(F32) == position, 1.0, 0.0).astype(BF16)
-    places = jnp.broadcast_to(column(place.astype(F32)), (ROWS, 128 - KB))
-    values = jnp.concatenate([amp_ref[...].T, places], axis=1)
-    packed = exact_pick(onehot, values)
+    places = jnp.broadcast_to(place.astype(F32), (128 - KB, ROWS))
+    values = jnp.concatenate([amp_ref[...], places], axis=0)
+    packed = exact_dot(
+        lambda part: lax.dot_general(onehot, part, (((1,), (1,)), ((), ())), preferred_element_type=F32), values
+    )
     out_ref[:ROWS, :] = packed
     out_ref[ROWS:, :] = packed
 
@@ -48,13 +49,12 @@
     places = arrived_ref[:ROWS, KB : KB + 1]
     along = lax.broadcasted_iota(jnp.int32, (ROWS, ROWS), 1).astype(F32)
     onehot = jnp.where(along == places, 1.0, 0.0).astype(BF16)
-    flipped = jnp.concatenate([arrived_ref[:ROWS, :].T[:KB], arrived_ref[ROWS:, :].T[:KB]])
-    hi = flipped.astype(BF16)
-    rest = flipped - hi.astype(F32)
-    mid = rest.astype(BF16)
-    lo = (rest - mid.astype(F32)).astype(BF16)
-    dot = lambda part: jnp.dot(part, onehot, preferred_element_type=F32)
-    out_ref[...] = (dot(hi) + dot(mid)) + dot(lo)
+    values = jnp.concatenate([arrived_ref[:ROWS, :], arrived_ref[ROWS:, :]], axis=1)
+    placed = exact_dot(
+        lambda part: lax.dot_general(part, onehot, (((0,), (0,)), ((), ())), preferred_element_type=F32), values
+    )
+    out_ref[:KB, :] = placed[:KB]
+    out_ref[KB:, :] = placed[128 : 128 + KB]
 
 
 def split(v):

time: 129 us -> 129 us (level)
  no operation moved by 1% of the time
where the time goes in v5:
time: 129 us
  blocking collectives  78.7 us (61%)
  waiting for transfers between devices  16.7 us (13%)
  Pallas kernels  16.5 us (13%)
  between operations  13.4 us (10%)
  starting transfers between devices  1.91 us (1%)
  local copies, waits for them, and re-layouts  1.46 us (1%)
    all_to_all x1, blocking collectives, local(): lax.all_to_all(spread, ('y_hi', 'x'), split_axis=0, concat_axis=0, tiled=...  60.2 us
    all_to_all x1, blocking collectives, local(): lax.all_to_all(outgoing, ('y_lo', 'y_hi', 'x', 'core'), split_axis=0, con...  18.5 us
    all_gather x1, waiting for transfers between devices, local(): amp = lax.all_gather(mine, 'z', axis=0, tiled=False)  16.6 us
    pallas_call x1, Pallas kernels, local(): pl.pallas_call(multiply_kernel, out_shape=jax.ShapeDtypeStruct((ROWS, COL...  12 us
  transfers between devices with their start and end apart: 2, of which 1 were waited for; matrix products, arithmetic and copies ran while one was open for 1% of the time, Pallas kernels for 0%

profile of v5, /device:TPU:4, one launch (start us, length us, event | category | flops | bytes accessed | tf_op | source)
XLA Modules:
  0.0 128.7 jit_solution(9029388153768207653)
XLA Ops:
  6.5 0.0 all-gather.3.cloned.1.call-start
  6.5 2.2 %shard_map.37 = f32[768,128]{1,0:T(8,128)} custom-call(s32[384]{0:T(512)} %rows_ref.1, f32[96,384]{1,0:T(8,128)} %bitcast.9), custom_call_target="tpu_custom_call" | custom-call | tf_op jit(solution)/shard_map/pallas_call | solution.py:107
  8.7 18.5 %all_to_all.16 = f32[32,24,128]{2,1,0:T(8,128)} all-to-all(f32[32,24,128]{2,1,0:T(8,128)} %bitcast.7), channel_id=1, replica_groups=mesh['y_hi'=2,'x'=4,'core'=2,'y_lo'=2,'z'=16] {'y_lo','y_hi','x','core'}, dimensions={0} | all-to-all | bytes 786432 | tf_op jit(solution)/shard_map/all_to_all | solution.py:113
  27.2 2.3 %shard_map.38 = f32[192,384]{1,0:T(8,128)} custom-call(f32[768,128]{1,0:T(8,128)} %bitcast.8), custom_call_target="tpu_custom_call" | custom-call | tf_op jit(solution)/shard_map/pallas_call | solution.py:114
  29.5 0.0 all-gather.3.cloned.1.call-update
  29.6 1.5 %broadcast_in_dim.10 = f32[8,192,768]{2,1,0:T(8,128)S(1)} broadcast(f32[192,768]{1,0:T(8,128)} %param.5), dimensions={1,2} | broadcast | bytes 5308416 | tf_op jit(solution)/shard_map/broadcast_in_dim | solution.py:123
  31.0 60.2 %all_to_all.17 = f32[8,192,768]{2,1,0:T(8,128)} all-to-all(f32[8,192,768]{2,1,0:T(8,128)S(1)} %broadcast_in_dim.10), channel_id=1, replica_groups=mesh['y_hi'=2,'x'=4,'core'=2,'y_lo'=2,'z'=16] {'y_hi','x'}, dimensions={0} | all-to-all | bytes 9437184 | tf_op jit(solution)/shard_map/all_to_all | solution.py:124
  91.2 1.9 %collective-permute-start = (f32[8,192,768]{2,1,0:T(8,128)}, f32[8,192,768]{2,1,0:T(8,128)}, u32[]{:S(2)}, u32[]{:S(2)}) collective-permute-start(f32[8,192,768]{2,1,0:T(8,128)} %all_to_all.17), channel_id=1, source_target_pairs={{0,32},{32,0},{1,33},{33,1},{2,34},{34,2},{3,35},{35,3},{4,36},{36... | collective-permute-start | bytes 14155784 | tf_op jit(solution)/shard_map/ppermute | solution.py:103
  93.1 16.6 %all-gather.3.cloned.1.call-done = f32[3072,384]{1,0:T(8,128)} async-done(((f32[192,384]{1,0:T(8,128)}), f32[3072,384]{1,0:T(8,128)}) %all-gather.3.cloned.1.call-update) | async-done | bytes 4718608 | tf_op jit(solution)/shard_map/all_gather | solution.py:120
  109.8 0.0 collective-permute-done
  109.8 12.0 %shard_map.39 = f32[384,768]{1,0:T(8,128)} custom-call(s32[1]{0:T(128)} %bitcast.core_ref, f32[16,192,384]{2,1,0:T(8,128)} %bitcast.10, f32[1536,768]{1,0:T(8,128)} %bitcast.5.refs_0_, f32[1536,768]{1,0:T(8,128)} %bitcast.6.refs_1_), custom_call_target="tpu_custom_call" | custom-call | flops 5435817984 | bytes 15728640 | tf_op jit(solution)/shard_map/pallas_call | solution.py:127
Async XLA Ops:
  6.5 103.3 %all-gather.3.cloned.1.call-start = ((), (), s32[]{:S(2)}) async-start(), calls=%async_computation.2 | async-start | bytes 5013504 | tf_op jit(solution)/shard_map/all_gather | solution.py:120
  91.2 18.6 %collective-permute-start = (f32[8,192,768]{2,1,0:T(8,128)}, f32[8,192,768]{2,1,0:T(8,128)}, u32[]{:S(2)}, u32[]{:S(2)}) collective-permute-start(f32[8,192,768]{2,1,0:T(8,128)} %all_to_all.17), channel_id=1, source_target_pairs={{0,32},{32,0},{1,33},{33,1},{2,34},{34,2},{3,35},{35,3},{4,36},{36... | collective-permute-start | bytes 14155784 | tf_op jit(solution)/shard_map/ppermute | solution.py:103
Sparse Core Ops, SparseCore 0:
  29.7 80.0 all-gather.2

commit v6 on v5

--- a/solution.py
+++ b/solution.py
@@ -84,15 +84,19 @@
     for i in range(4):
         for copy in [ints_copy(i)] + amp_copies(i):
             copy.start()
-    for i in range(4):
-        here = slice(i * 4 * KR, (i + 1) * 4 * KR)
-        for copy in amp_copies(i):
-            copy.wait()
-        amp_hi[here, :], amp_lo[here, :] = split(amp[8 * i : 8 * i + 8].reshape(4 * KR, ROWS))
-        ints_copy(i).wait()
-        ints_hi[here, :], ints_lo[here, :] = split(ints[i])
-    dot = lambda a, b: lax.dot_general(a[...], b[...], (((0,), (0,)), ((), ())), preferred_element_type=F32)
-    out_ref[...] = dot(amp_hi, ints_hi) + (dot(amp_hi, ints_lo) + dot(amp_lo, ints_hi))
+    dot = lambda a, b: lax.dot_general(a, b, (((0,), (0,)), ((), ())), preferred_element_type=F32)
+    for first, last in ((0, 3), (3, 4)):
+        for i in range(first, last):
+            here = slice(i * 4 * KR, (i + 1) * 4 * KR)
+            for copy in amp_copies(i):
+                copy.wait()
+            amp_hi[here, :], amp_lo[here, :] = split(amp[8 * i : 8 * i + 8].reshape(4 * KR, ROWS))
+            ints_copy(i).wait()
+            ints_hi[here, :], ints_lo[here, :] = split(ints[i])
+        here = slice(first * 4 * KR, last * 4 * KR)
+        a_hi, a_lo, b_hi, b_lo = amp_hi[here, :], amp_lo[here, :], ints_hi[here, :], ints_lo[here, :]
+        part = dot(a_hi, b_hi) + (dot(a_hi, b_lo) + dot(a_lo, b_hi))
+        out_ref[...] = part if first == 0 else out_ref[...] + part
 
 
 def vmem(n):

time: 129 us -> 129 us (level)
  no operation moved by 1% of the time
where the time goes in v6:
time: 129 us
  blocking collectives  78.7 us (61%)
  Pallas kernels  16.8 us (13%)
  waiting for transfers between devices  16.7 us (13%)
  between operations  13.4 us (10%)
  starting transfers between devices  1.91 us (1%)
  local copies, waits for them, and re-layouts  1.46 us (1%)
    all_to_all x1, blocking collectives, local(): lax.all_to_all(spread, ('y_hi', 'x'), split_axis=0, concat_axis=0, tiled=...  60.2 us
    all_to_all x1, blocking collectives, local(): lax.all_to_all(outgoing, ('y_lo', 'y_hi', 'x', 'core'), split_axis=0, con...  18.5 us
    all_gather x1, waiting for transfers between devices, local(): amp = lax.all_gather(mine, 'z', axis=0, tiled=False)  16.6 us
    pallas_call x1, Pallas kernels, local(): pl.pallas_call(multiply_kernel, out_shape=jax.ShapeDtypeStruct((ROWS, COL...  12.3 us
  transfers between devices with their start and end apart: 2, of which 1 were waited for; matrix products, arithmetic and copies ran while one was open for 1% of the time, Pallas kernels for 0%

profile of v6, /device:TPU:4, one launch (start us, length us, event | category | flops | bytes accessed | tf_op | source)
XLA Modules:
  0.0 128.9 jit_solution(7587297672748590904)
XLA Ops:
  6.5 0.0 all-gather.3.cloned.1.call-start
  6.5 2.2 %shard_map.37 = f32[768,128]{1,0:T(8,128)} custom-call(s32[384]{0:T(512)} %rows_ref.1, f32[96,384]{1,0:T(8,128)} %bitcast.9), custom_call_target="tpu_custom_call" | custom-call | tf_op jit(solution)/shard_map/pallas_call | solution.py:111
  8.7 18.5 %all_to_all.16 = f32[32,24,128]{2,1,0:T(8,128)} all-to-all(f32[32,24,128]{2,1,0:T(8,128)} %bitcast.7), channel_id=1, replica_groups=mesh['y_hi'=2,'x'=4,'core'=2,'y_lo'=2,'z'=16] {'y_lo','y_hi','x','core'}, dimensions={0} | all-to-all | bytes 786432 | tf_op jit(solution)/shard_map/all_to_all | solution.py:117
  27.2 2.3 %shard_map.38 = f32[192,384]{1,0:T(8,128)} custom-call(f32[768,128]{1,0:T(8,128)} %bitcast.8), custom_call_target="tpu_custom_call" | custom-call | tf_op jit(solution)/shard_map/pallas_call | solution.py:118
  29.5 0.0 all-gather.3.cloned.1.call-update
  29.6 1.5 %broadcast_in_dim.10 = f32[8,192,768]{2,1,0:T(8,128)S(1)} broadcast(f32[192,768]{1,0:T(8,128)} %param.5), dimensions={1,2} | broadcast | bytes 5308416 | tf_op jit(solution)/shard_map/broadcast_in_dim | solution.py:127
  31.0 60.2 %all_to_all.17 = f32[8,192,768]{2,1,0:T(8,128)} all-to-all(f32[8,192,768]{2,1,0:T(8,128)S(1)} %broadcast_in_dim.10), channel_id=1, replica_groups=mesh['y_hi'=2,'x'=4,'core'=2,'y_lo'=2,'z'=16] {'y_hi','x'}, dimensions={0} | all-to-all | bytes 9437184 | tf_op jit(solution)/shard_map/all_to_all | solution.py:128
  91.2 1.9 %collective-permute-start = (f32[8,192,768]{2,1,0:T(8,128)}, f32[8,192,768]{2,1,0:T(8,128)}, u32[]{:S(2)}, u32[]{:S(2)}) collective-permute-start(f32[8,192,768]{2,1,0:T(8,128)} %all_to_all.17), channel_id=1, source_target_pairs={{0,32},{32,0},{1,33},{33,1},{2,34},{34,2},{3,35},{35,3},{4,36},{36... | collective-permute-start | bytes 14155784 | tf_op jit(solution)/shard_map/ppermute | solution.py:107
  93.1 16.6 %all-gather.3.cloned.1.call-done = f32[3072,384]{1,0:T(8,128)} async-done(((f32[192,384]{1,0:T(8,128)}), f32[3072,384]{1,0:T(8,128)}) %all-gather.3.cloned.1.call-update) | async-done | bytes 4718608 | tf_op jit(solution)/shard_map/all_gather | solution.py:124
  109.8 0.0 collective-permute-done
  109.8 12.3 %shard_map.39 = f32[384,768]{1,0:T(8,128)} custom-call(s32[1]{0:T(128)} %bitcast.core_ref, f32[16,192,384]{2,1,0:T(8,128)} %bitcast.10, f32[1536,768]{1,0:T(8,128)} %bitcast.5.refs_0_, f32[1536,768]{1,0:T(8,128)} %bitcast.6.refs_1_), custom_call_target="tpu_custom_call" | custom-call | flops 5435817984 | bytes 15728640 | tf_op jit(solution)/shard_map/pallas_call | solution.py:131
Async XLA Ops:
  6.5 103.3 %all-gather.3.cloned.1.call-start = ((), (), s32[]{:S(2)}) async-start(), calls=%async_computation.2 | async-start | bytes 5013504 | tf_op jit(solution)/shard_map/all_gather | solution.py:124
  91.2 18.6 %collective-permute-start = (f32[8,192,768]{2,1,0:T(8,128)}, f32[8,192,768]{2,1,0:T(8,128)}, u32[]{:S(2)}, u32[]{:S(2)}) collective-permute-start(f32[8,192,768]{2,1,0:T(8,128)} %all_to_all.17), channel_id=1, source_target_pairs={{0,32},{32,0},{1,33},{33,1},{2,34},{34,2},{3,35},{35,3},{4,36},{36... | collective-permute-start | bytes 14155784 | tf_op jit(solution)/shard_map/ppermute | solution.py:107
Sparse Core Ops, SparseCore 0:
  29.7 80.0 all-gather.2
